TPU v7x, 512 devices: a whole 4x8x8 slice. The times are simulated.
512 devices in a mesh: ctx: 32 (over y_hi, z), tp: 16 (over y_lo, x, core).
Axes of the slice: x: 4, y: 8 (y_hi: 4, y_lo: 2; y = y_hi * 2 + y_lo), z: 8, core: 2. Of those that a mesh axis runs over, the one named last changes fastest.
Arguments:
- queries: bfloat16 [4096, 8192], P('ctx', 'tp'), may hold values from -56 to 56
- suffix_kv: bfloat16 [2, 4096, 2048], P(None, 'ctx', 'tp'), may hold values from -6 to 6
- cache_pool: bfloat16 [2, 512, 128, 2048], P(None, 'ctx', None, 'tp'), may hold values from -6 to 6
- hit_count: int32 [32], replicated, may hold values from 1 to 3, as said below
- hit_slots: int32 [32, 3], P('ctx'), may hold values from 0 to 15, as said below
- out_weight: bfloat16 [8192, 8192], P('tp', 'ctx'), may hold values from -1.1953125 to 1.1953125
Outputs:
- layer_out: bfloat16 [4096, 8192], P('tp', 'ctx')
Inputs may be any that keep to these rules, and one draw needn't show every extreme that they name: hit_count[h] blocks of holder h belong to the prefix; some holder has exactly 3. `hit_slots`: row h names 3 distinct slots of holder h's pool; only its first hit_count[h] entries are hits, the others are unused.
All inputs are finite; a program needn't handle non-finite values.
Results may differ from a plain program's by a relative error of at most 0.024.
Values may be sent and summed in bfloat16 or wider, within the bound.
A program may use at most 64 MiB of HBM per device.

v0:
```python
import math

import jax
import jax.numpy as jnp
from jax import lax
from jax.sharding import PartitionSpec as P

HD = 128
HCAP = 3


neg_fill = -1e30
blocks_per_turn = 4


def begin_state(query_count, slots_dev, group_size, head_width):
    return (
        jnp.full((query_count, slots_dev, group_size), neg_fill, jnp.float32),
        jnp.zeros((query_count, slots_dev, group_size), jnp.float32),
        jnp.zeros((query_count, slots_dev, group_size, head_width), jnp.float32),
    )


def absorb(softmax_state, query_heads, key_block, visible):
    running_max, running_sum, running_acc = softmax_state
    slots_dev = query_heads.shape[1]
    head_width = query_heads.shape[3]
    key_count = key_block.shape[1]
    key_rows = key_block[0].reshape(key_count, slots_dev, head_width)
    value_rows = key_block[1].reshape(key_count, slots_dev, head_width)
    scores = jnp.einsum(
        "qsgd,ksd->qsgk", query_heads, key_rows, preferred_element_type=jnp.float32
    ) / math.sqrt(head_width)
    mask_all = visible[:, None, None, :]
    scores = jnp.where(mask_all, scores, neg_fill)
    new_max = jnp.maximum(running_max, jnp.max(scores, axis=-1))
    weights = jnp.where(mask_all, jnp.exp(scores - new_max[..., None]), 0.0)
    rescale = jnp.exp(running_max - new_max)
    new_sum = running_sum * rescale + jnp.sum(weights, axis=-1)
    rounded_weights = weights.astype(jnp.bfloat16)
    new_acc = running_acc * rescale[..., None] + jnp.einsum(
        "qsgk,ksd->qsgd", rounded_weights, value_rows, preferred_element_type=jnp.float32
    )
    return (new_max, new_sum, new_acc)


def prefix_visible(slot_index, hit_count):
    holder = slot_index // HCAP
    within = slot_index % HCAP
    holders = jnp.arange(hit_count.shape[0], dtype=jnp.int32)
    counted = jnp.sum(jnp.where(holder[:, None] == holders[None, :], hit_count[None, :], 0), axis=1)
    return within < counted


def body(queries, suffix_kv, cache_pool, hit_count, hit_slots, out_weight):
    tok_rows = queries.shape[0]
    slots_dev = suffix_kv.shape[2] // HD
    heads_dev = queries.shape[1] // HD
    group_size = heads_dev // slots_dev
    query_heads = queries.reshape(tok_rows, slots_dev, group_size, HD)
    my_index = lax.axis_index("ctx")
    query_pos = my_index * tok_rows + jnp.arange(tok_rows, dtype=jnp.int32)
    last_query = my_index * tok_rows + tok_rows - 1
    block_rows = cache_pool.shape[2]
    row_width = cache_pool.shape[3]
    picked = jnp.take(cache_pool, hit_slots[0], axis=1)
    initial = begin_state(tok_rows, slots_dev, group_size, HD)
    fragment = lax.all_gather(picked, "ctx", axis=1, tiled=True)
    slot_count = fragment.shape[1]
    step_size = math.gcd(slot_count, blocks_per_turn * HCAP)
    flattened = fragment.reshape(2, slot_count * block_rows, row_width)

    def advance(position, current):
        key_block = lax.dynamic_slice_in_dim(
            flattened, position * step_size * block_rows, step_size * block_rows, 1
        )
        slot_index = (
            position * step_size + jnp.arange(step_size * block_rows, dtype=jnp.int32) // block_rows
        )
        visible = prefix_visible(slot_index, hit_count)[None, :]
        return absorb(current, query_heads, key_block, visible)

    after_prefix = lax.fori_loop(0, slot_count // step_size, advance, initial)
    fragment = lax.all_gather(suffix_kv, "ctx", axis=1, tiled=True)
    row_count = fragment.shape[1]
    fold_step_size = math.gcd(row_count, blocks_per_turn * tok_rows)

    def advance(position, current):
        first_key = position * fold_step_size

        def include(running):
            key_block = lax.dynamic_slice_in_dim(
                fragment, position * fold_step_size, fold_step_size, 1
            )
            key_pos = first_key + jnp.arange(fold_step_size, dtype=jnp.int32)
            return absorb(running, query_heads, key_block, key_pos[None, :] <= query_pos[:, None])

        return lax.cond(first_key <= last_query, include, lambda running: running, current)

    final_state = lax.fori_loop(0, row_count // fold_step_size, advance, after_prefix)
    running_max, running_sum, running_acc = final_state
    attention = (
        (running_acc / running_sum[..., None])
        .reshape(tok_rows, heads_dev * HD)
        .astype(jnp.bfloat16)
    )
    gathered = lax.all_gather(attention, "ctx", axis=0, tiled=True)
    return lax.psum_scatter(
        jnp.dot(gathered, out_weight, preferred_element_type=jnp.float32).astype(jnp.bfloat16),
        "tp",
        scatter_dimension=0,
        tiled=True,
    )


def solution(mesh):
    placed = (
        P("ctx", "tp"),
        P(None, "ctx", "tp"),
        P(None, "ctx", None, "tp"),
        P(),
        P("ctx", None),
        P("tp", "ctx"),
    )
    return jax.shard_map(
        body, mesh=mesh, in_specs=placed, out_specs=P("tp", "ctx"), check_vma=False
    )
```

profile of v0, /device:TPU:16, one launch (start us, length us, event | category | flops | bytes accessed | tf_op | source)
XLA Modules:
  0.0 419.8 jit_solution(2069720989467839405)
XLA Ops:
  11.4 122.6 %all-gather.4.cloned.1.call-done = bf16[2,96,128,128]{3,2,0,1:T(8,128)(2,1)} async-done(((bf16[2,3,128,128]{3,2,0,1:T(8,128)(2,1)}), bf16[2,96,128,128]{3,2,0,1:T(8,128)(2,1)}) %all-gather.4.cloned.1.call-update) | async-done | bytes 6291472 | tf_op jit(solution)/shard_map/all_gather | solution.py:68
  133.9 8.1 %copy.39 = bf16[2,96,128,128]{3,2,1,0:T(8,128)(2,1)} copy(bf16[2,96,128,128]{3,2,0,1:T(8,128)(2,1)} %all-gather.4.cloned.1.call-done) | data formatting | bytes 12582912 | tf_op jit(solution)/shard_map/all_gather | solution.py:68
  142.0 56.4 %while.40 = (s32[]{:T(128)}, f32[128,1,4]{0,2,1:T(4,128)S(1)}, f32[128,1,4]{0,2,1:T(4,128)S(1)}, f32[128,1,4,128]{0,3,2,1:T(8,128)S(1)}, s32[32]{0:T(128)S(1)}, ...) while((s32[]{:T(128)}, f32[128,1,4]{0,2,1:T(4,128)S(1)}, ...), condition=%wide.region_4.5_spmd.clone, body=%wide.region_0.4_spmd.clone.sunk | while | flops 410127360 | bytes 23525756 | solution.py:83
  142.2 3.3 bitcast_reduce_fusion.2
  145.5 2.9 fusion.66
  149.2 3.3 bitcast_reduce_fusion.2
  152.5 2.9 fusion.66
  156.2 3.3 bitcast_reduce_fusion.2
  163.3 3.3 bitcast_reduce_fusion.2
  170.3 3.3 bitcast_reduce_fusion.2
  173.6 2.9 fusion.66
  177.3 3.3 bitcast_reduce_fusion.2
  180.6 2.9 fusion.66
  184.4 3.3 bitcast_reduce_fusion.2
  187.7 3.1 fusion.66
  191.5 3.3 bitcast_reduce_fusion.2
  198.4 22.6 %all-gather.6.cloned.1.call-done = bf16[2,4096,128]{2,1,0:T(8,128)(2,1)} async-done(((bf16[2,128,128]{2,1,0:T(8,128)(2,1)}), bf16[2,4096,128]{2,1,0:T(8,128)(2,1)}) %all-gather.6.cloned.1.call-update) | async-done | bytes 2097168 | tf_op jit(solution)/shard_map/all_gather | solution.py:84
  221.0 9.2 %while.39 = (s32[]{:T(128)}, f32[128,1,4]{0,2,1:T(4,128)S(1)}, f32[128,1,4]{0,2,1:T(4,128)S(1)}, f32[128,1,4,128]{0,3,2,1:T(8,128)S(1)}, s32[]{:T(128)}, /*index...) while((s32[]{:T(128)}, f32[128,1,4]{0,2,1:T(4,128)S(1)}, ...), condition=%wide.region_10.11_spmd.clone, body=%wide.region_5.10_spmd.clone.sunk | while | flops 136775808 | bytes 4364621 | solution.py:100
  221.0 2.9 conditional.3
  224.0 3.0 conditional.3
  227.0 3.0 conditional.3
  231.0 109.8 %all-gather.8.cloned.1.call-done = bf16[4096,512]{0,1:T(8,128)(2,1)} async-done(((bf16[128,512]{0,1:T(8,128)(2,1)}), bf16[4096,512]{0,1:T(8,128)(2,1)}) %all-gather.8.cloned.1.call-update) | async-done | bytes 4194320 | tf_op jit(solution)/shard_map/all_gather | solution.py:107
  340.8 4.8 %convolution_convert_fusion = bf16[4096,256]{1,0:T(8,128)(2,1)} fusion(bf16[4096,512]{0,1:T(8,128)(2,1)} %all-gather.8.cloned.1.call-done, bf16[512,256]{1,0:T(8,128)(2,1)S(1)} %copy-done.3), kind=kOutput, calls=%fused_computation.76 | convolution fusion | flops 1074790400 | bytes 6553600 | tf_op jit(solution)/shard_map/dot_general | solution.py:109
  345.6 67.6 %reduce-scatter.2.cloned.1.call-done = bf16[256,256]{1,0:T(8,128)(2,1)} async-done(((bf16[4096,256]{1,0:T(8,128)(2,1)}), bf16[256,256]{1,0:T(8,128)(2,1)}) %reduce-scatter.2.cloned.1.call-update) | async-done | bytes 131088 | tf_op jit(solution)/shard_map/reduce_scatter | solution.py:108
  (140 shorter events, 29.2 us)
Async XLA Ops:
  6.5 1.4 copy-start
  6.5 127.4 %all-gather.4.cloned.1.call-start = ((), (), s32[]{:S(2)}) async-start(), calls=%async_computation.1 | async-start | bytes 6488064 | tf_op jit(solution)/shard_map/all_gather | solution.py:68
  9.3 211.7 %all-gather.6.cloned.1.call-start = ((), (), s32[]{:S(2)}) async-start(), calls=%async_computation.2 | async-start | bytes 2162688 | tf_op jit(solution)/shard_map/all_gather | solution.py:84
  10.1 330.7 %all-gather.8.cloned.1.call-start = ((), (), s32[]{:S(2)}) async-start(), calls=%async_computation.3 | async-start | bytes 4325376 | tf_op jit(solution)/shard_map/all_gather | solution.py:107
  11.3 130.7 %copy-start.2 = (s32[32]{0:T(128)S(1)}, s32[32]{0:T(128)}, u32[]{:S(2)}) copy-start(s32[32]{0:T(128)} %param.15) | copy-start | bytes 388
  145.5 3.0 copy-start.1
  152.5 3.0 copy-start.1
  159.5 3.0 copy-start.1
  166.6 3.0 copy-start.1
  173.6 3.0 copy-start.1
  180.6 3.0 copy-start.1
  187.7 3.1 copy-start.1
  194.8 3.0 copy-start.1
  221.0 119.8 %copy-start.3 = (bf16[512,256]{1,0:T(8,128)(2,1)S(1)}, bf16[512,256]{1,0:T(8,128)(2,1)}, u32[]{:S(2)}) copy-start(bf16[512,256]{1,0:T(8,128)(2,1)} %param.17) | copy-start | bytes 786436
  230.9 182.3 %reduce-scatter.2.cloned.1.call-start = ((), (), s32[]{:S(2)}) async-start(), calls=%async_computation.4 | async-start | bytes 2228224 | tf_op jit(solution)/shard_map/reduce_scatter | solution.py:108
Sparse Core Ops, SparseCore 0:
  10.5 123.3 all-gather.3
  137.1 83.8 all-gather.5
  231.1 109.6 all-gather.7
  345.8 67.4 reduce-scatter.1
where the time goes:
time: 421 us; the launch traced here: 420 us
  waiting for transfers between devices  323 us (77%)
  matrix products  62.2 us (15%)
  between operations  13.2 us (3%)
  local copies, waits for them, and re-layouts  10.2 us (2%)
  other arithmetic  9.93 us (2%)
    all_gather x1, waiting for transfers between devices, body(): fragment = lax.all_gather(picked, 'ctx', axis=1, tiled=True)  123 us
    all_gather x1, waiting for transfers between devices, body(): gathered = lax.all_gather(attention, 'ctx', axis=0, tiled=True)  110 us
    reduce_scatter x1, waiting for transfers between devices, body(): lax.psum_scatter(jnp.dot(gathered, out_weight, preferred_element_type=jnp...  67.6 us
    dot_general x11, matrix products, absorb(): jnp.einsum('qsgd,ksd->qsgk', query_heads, key_rows, preferred_element_typ...  29.9 us
    dot_general x11, matrix products, absorb(): jnp.einsum('qsgk,ksd->qsgd', rounded_weights, value_rows, preferred_eleme...  27.4 us
    all_gather x1, waiting for transfers between devices, body(): fragment = lax.all_gather(suffix_kv, 'ctx', axis=1, tiled=True)  22.6 us
  transfers between devices with their start and end apart: 4, of which 4 were waited for; matrix products, arithmetic and copies ran while one was open for 15% of the time, Pallas kernels for 0%

commit v1 on v0

v1 whole, which is shorter than its diff:
```python
import math

import jax
import jax.numpy as jnp
from jax import lax
from jax.experimental import pallas as pl
from jax.experimental.pallas import tpu as pltpu
from jax.sharding import PartitionSpec as P

HD = 128
HCAP = 3
BLK = 128
YH, NZ, YL, NX, CORES = 4, 8, 2, 4, 2
HEADS = 4
TOK = 128
KEYS = HCAP * BLK + TOK
HALF = TOK // CORES
WIDTH = HEADS * HD
COLS = 256
NEG = -1e30
SCALE = math.log2(math.e) / math.sqrt(HD)
Y_STEP = (0, 3, 1, 2)
Z_STEP = (0, 7, 1, 6, 2, 5, 3, 4)
MESH = pl.DeviceIdType.MESH
F32 = jnp.float32
BF16 = jnp.bfloat16


def at(yh, z, yl, x, core):
    return (yh * NZ + z, yl * (NX * CORES) + x * CORES + core)


def kernel(
    q_ref, k_ref, v_ref, w_ref, count_ref, o_ref,
    kb, vb, qb, wb, acc, mx, ob, st, rob, rst, wt, ab, cb, rb, fb, fin,
    k_ss, k_rs, q_ss, q_rs, w_ss, w_rs, s_ss, s_rs, o_ss, o_rs, t_ss, t_rs, a_ss, a_rs,
    c_ss, c_rs, f_ss, f_rs,
):
    c_index = lax.axis_index("ctx")
    t_index = lax.axis_index("tp")
    yh, z = c_index // NZ, c_index % NZ
    yl, x, core = t_index // (NX * CORES), (t_index // CORES) % NX, t_index % CORES
    chip = yl * NX + x
    other = 1 - core
    z_right, z_left = at(yh, (z + 1) % NZ, yl, x, core), at(yh, (z + NZ - 1) % NZ, yl, x, core)
    y_right, y_left = at((yh + 1) % YH, z, yl, x, core), at((yh + YH - 1) % YH, z, yl, x, core)
    sibling = at(yh, z, yl, x, other)

    def remote(src, dst, send, recv, device):
        return pltpu.make_async_remote_copy(
            src_ref=src, dst_ref=dst, send_sem=send, recv_sem=recv,
            device_id=device, device_id_type=MESH,
        )

    y_tok = yl * 2 + x // 2
    step_in = (yh + YH - y_tok) % YH
    in_yl = (y_tok // 2 + ((step_in + 1) // 2 + 1)) % 2
    in_x = ((y_tok % 2 + 1 - step_in // 2) % 2) * 2 + x % 2

    g1 = (yl + yh // 2) % 2
    g0 = (x // 2 + yh % 2) % 2
    step_out = (1 - g1) * (2 - g0) + g1 * 3 * (1 - g0)
    out_y = (yh + step_out) % YH

    def out_device(to_core):
        return at(out_y, z, yh // 2, (yh % 2) * 2 + x % 2, to_core)

    barrier = pltpu.get_barrier_semaphore()
    greeted = [z_right, z_left, sibling]
    for step in range(1, YH):
        for to_core in range(CORES):
            greeted.append(at((yh + step) % YH, z, yl, x, to_core))
    for dy in range(YL):
        for dx in range(NX):
            if (dy, dx) != (0, 0):
                greeted.append(at(yh, z, (yl + dy) % YL, (x + dx) % NX, core))
    for from_core in range(CORES):
        greeted.append(at(y_tok, z, in_yl, in_x, from_core))
    for device in greeted:
        pl.semaphore_signal(barrier, inc=1, device_id=device, device_id_type=MESH)
    pl.semaphore_wait(barrier, len(greeted))

    def kv_copy(slot, which):
        buf = (kb, vb)[which]
        if slot == 7:
            source, device = (5, z_right) if which == 0 else (6, z_left)
        else:
            source, device = max(slot - 2, 0), z_right if slot % 2 else z_left
        return remote(
            buf.at[source], buf.at[slot], k_ss.at[slot, which], k_rs.at[slot, which], device
        )

    def a_copy(slot, which):
        if slot == 7:
            source, device = (5, z_right) if which == 0 else (6, z_left)
        else:
            source, device = max(slot - 2, 0), z_right if slot % 2 else z_left
        return remote(
            ab.at[source, which], ab.at[slot, which],
            a_ss.at[slot, which], a_rs.at[slot, which], device,
        )

    def y_copy(buf, ss, rs, slot, half):
        rows = pl.ds(half * (WIDTH // 2), WIDTH // 2)
        if slot == 3:
            source, device = (1, y_right) if half == 0 else (2, y_left)
        else:
            source, device = 0, y_right if slot == 1 else y_left
        return remote(
            buf.at[source, rows], buf.at[slot, rows], ss.at[slot, half], rs.at[slot, half], device
        )

    def q_copy(slot, half):
        return y_copy(qb, q_ss, q_rs, slot, half)

    def w_copy(slot, half):
        return y_copy(wb.at[0], w_ss, w_rs, slot, half)

    def sib_copy(slot):
        return remote(wb.at[0, slot], wb.at[1, slot], s_ss.at[slot], s_rs.at[slot], sibling)

    row_minus_col = lax.broadcasted_iota(jnp.int32, (2 * TOK, TOK), 0) % TOK - (
        lax.broadcasted_iota(jnp.int32, (2 * TOK, TOK), 1)
    )

    def absorb(q_slot, step_y, slot, count, step_z):
        ones = []
        gaps = []
        for i in range(count):
            z_key = (z + step_z[i]) % NZ
            hits = count_ref[yh * NZ + z_key]
            for b in range(HCAP):
                ones.append(jnp.full((BLK, HD), jnp.where(b < hits, 1.0, 0.0), F32).astype(BF16))
            ones.append(jnp.ones((TOK, HD), BF16))
            gaps.append(((yh + step_y) % YH * NZ + z - yh * NZ - z_key) * TOK)
        ones = jnp.concatenate(ones, axis=0)
        keys = kb[slot : slot + count].reshape(count * KEYS, HD)
        values = jnp.concatenate([vb[slot : slot + count].reshape(count * KEYS, HD), ones], axis=1)

        @pl.loop(0, HEADS // 2)
        def _(pair):
            rows = pl.ds(pl.multiple_of(pair * 2 * TOK, 2 * TOK), 2 * TOK)
            scores = lax.dot_general(
                qb[q_slot, rows, :], keys, (((1,), (1,)), ((), ())), preferred_element_type=F32
            )
            parts = []
            for i in range(count):
                parts.append(scores[:, i * KEYS : i * KEYS + HCAP * BLK])
                own = scores[:, i * KEYS + HCAP * BLK : (i + 1) * KEYS]
                parts.append(jnp.where(row_minus_col + gaps[i] >= 0, own, NEG))
            scores = jnp.concatenate(parts, axis=1)
            before = mx[q_slot, rows, :]
            now = jnp.maximum(before, jnp.max(scores, axis=1, keepdims=True))
            mx[q_slot, rows, :] = now
            fade = jnp.exp2((before - now) * SCALE)
            weights = jnp.exp2((scores - now[:, :1]) * SCALE).astype(BF16)
            mixed = jnp.dot(weights, values, preferred_element_type=F32)
            acc[q_slot, rows, :] = (
                acc[q_slot, rows, :] * jnp.concatenate([fade, fade], axis=1) + mixed
            )

    kb[0] = k_ref[...]
    vb[0] = v_ref[...]
    for which in range(2):
        for slot in (1, 2):
            kv_copy(slot, which).start()
    for head in range(HEADS):
        qb[0, head * TOK : (head + 1) * TOK, :] = q_ref[:, head * HD : (head + 1) * HD]
    for slot, half in ((1, 0), (2, 1), (1, 1), (2, 0)):
        q_copy(slot, half).start()
    wb[0, 0] = w_ref[...]
    sib_copy(0).start()

    @pl.loop(0, YH)
    def _(slot):
        mx[slot] = jnp.full((WIDTH, HD), NEG, F32)
        acc[slot] = jnp.zeros((WIDTH, 2 * HD), F32)

    def pass_on(slot):
        for which in range(2):
            for s in (slot, slot + 1):
                kv_copy(s, which).wait_recv()
                if s + 2 < 7:
                    kv_copy(s + 2, which).start()
                elif (s, which) in ((5, 0), (6, 1)):
                    kv_copy(7, which).start()

    def y_step(slot):
        return (slot * 5 - slot * slot * 2) % YH if not isinstance(slot, int) else Y_STEP[slot]

    absorb(0, 0, 0, 1, Z_STEP[0:1])
    pass_on(1)
    absorb(0, 0, 1, 2, Z_STEP[1:3])
    q_copy(1, 0).wait_recv()
    q_copy(3, 0).start()
    q_copy(2, 1).wait_recv()
    q_copy(3, 1).start()
    q_copy(1, 1).wait_recv()
    q_copy(2, 0).wait_recv()
    for slot, half in ((1, 0), (2, 1), (1, 1), (2, 0)):
        w_copy(slot, half).start()
    pass_on(3)

    @pl.loop(1, 3)
    def _(slot):
        step = 3 - 2 * (slot - 1)
        absorb(slot, step, 0, 1, Z_STEP[0:1])
        absorb(slot, step, 1, 2, Z_STEP[1:3])

    @pl.loop(0, 3)
    def _(slot):
        absorb(slot, (slot * 3 + (slot // 2) * 3) % YH, 3, 2, Z_STEP[3:5])

    pass_on(5)
    q_copy(3, 0).wait_recv()
    q_copy(3, 1).wait_recv()
    absorb(3, 2, 0, 1, Z_STEP[0:1])
    absorb(3, 2, 1, 2, Z_STEP[1:3])
    absorb(3, 2, 3, 2, Z_STEP[3:5])

    @pl.loop(0, YH)
    def _(slot):
        absorb(slot, (slot * 3 + (slot // 2) * 3 + (slot // 3) * 2) % YH, 5, 2, Z_STEP[5:7])

    w_copy(1, 0).wait_recv()
    w_copy(3, 0).start()
    w_copy(2, 1).wait_recv()
    w_copy(3, 1).start()
    w_copy(1, 1).wait_recv()
    sib_copy(1).start()
    w_copy(2, 0).wait_recv()
    sib_copy(2).start()
    kv_copy(7, 0).wait_recv()
    kv_copy(7, 1).wait_recv()

    lane = lax.broadcasted_iota(jnp.int32, (TOK, HD), 1)

    def finish(slot):
        stats = jnp.ones((TOK, HD), F32)
        for head in range(HEADS):
            rows = slice(head * TOK, (head + 1) * TOK)
            total = acc[slot, rows, HD:]
            result = (acc[slot, rows, :HD] / total).astype(BF16)
            for half in range(CORES):
                ob[slot, half, :, head * HD : (head + 1) * HD] = (
                    result[half * HALF : (half + 1) * HALF]
                )
            stats = jnp.where(lane == head, mx[slot, rows, :] * SCALE, stats)
            stats = jnp.where(lane == 8 + head, total, stats)
        st[slot] = stats.T[:16, :]

    def o_copies(slot, which):
        to_core = (core, other)[which]
        device = at((yh + Y_STEP[slot]) % YH, z, yl, x, to_core)
        return (
            remote(
                st.at[slot], rst.at[which, slot], t_ss.at[slot, which], t_rs.at[slot, which], device
            ),
            remote(
                ob.at[slot, to_core], rob.at[which, slot],
                o_ss.at[slot, which], o_rs.at[slot, which], device,
            ),
        )

    for slot in (3, 1, 2, 0):
        absorb(slot, Y_STEP[slot], 7, 1, Z_STEP[7:8])
        finish(slot)
        for which in range(CORES):
            if (slot, which) != (0, 0):
                for copy in o_copies(slot, which):
                    copy.start()
    rst[0, 0] = st[0]
    rob[0, 0] = ob[0, core]
    w_copy(3, 0).wait_recv()
    w_copy(3, 1).wait_recv()
    sib_copy(3).start()
    for slot in (3, 1, 2, 0):
        for which in range(CORES):
            if (slot, which) != (0, 0):
                for copy in o_copies(slot, which):
                    copy.wait_recv()

    shares = []
    for which in range(CORES):
        top = rst[which, 0, :8]
        for slot in range(1, YH):
            top = jnp.maximum(top, rst[which, slot, :8])
        raw = [rst[which, slot, 8:] * jnp.exp2(rst[which, slot, :8] - top) for slot in range(YH)]
        whole = raw[0] + raw[1] + raw[2] + raw[3]
        shares += [share / whole for share in raw]
    wt[...] = jnp.concatenate(shares + shares, axis=0).T
    share = wt[pl.ds(pl.multiple_of(core * HALF, HALF), HALF), :]
    for which in range(CORES):
        for head in range(HEADS):
            columns = slice(head * HD, (head + 1) * HD)
            summed = jnp.zeros((HALF, HD), F32)
            for slot in range(YH):
                spot = (which * YH + slot) * 8 + head
                summed += share[:, spot : spot + 1] * rob[which, slot, :, columns].astype(F32)
            ab[0, which, :, columns] = summed.astype(BF16)
        for slot in (1, 2):
            a_copy(slot, which).start()

    def c_place(slot, w_slot):
        step = Y_STEP[w_slot]
        c1, c0 = ((1, 1), (0, 1), (0, 0), (1, 0))[step]
        z_tok = (z + Z_STEP[slot]) % NZ
        to_yl = (yh // 2 + c1) % 2
        to_x = ((yh % 2 + c0) % 2) * 2 + z_tok // 4
        return to_yl, to_x, z_tok % 4

    def c_copy(slot, w_slot):
        to_yl, to_x, spot = c_place(slot, w_slot)
        return remote(
            cb.at[slot, w_slot], rb.at[chip, spot],
            c_ss.at[slot, w_slot], c_rs.at[chip, spot], at(yh, z, to_yl, to_x, core),
        )

    def project(slot, count):
        left = [ab[slot : slot + count, which].reshape(count * HALF, WIDTH) for which in range(CORES)]
        for w_slot in (3, 1, 2, 0):
            part = jnp.dot(left[0], wb[0, w_slot], preferred_element_type=F32)
            part += jnp.dot(left[1], wb[1, w_slot], preferred_element_type=F32)
            part = part.astype(BF16)
            for i in range(count):
                cb[slot + i, w_slot] = part[i * HALF : (i + 1) * HALF]
                to_yl, to_x, spot = c_place(slot + i, w_slot)
                here = to_yl * NX + to_x == chip

                @pl.when(here)
                def _():
                    rb[chip, spot] = part[i * HALF : (i + 1) * HALF]

                @pl.when(jnp.logical_not(here))
                def _():
                    c_copy(slot + i, w_slot).start()

    for slot in range(YH):
        sib_copy(slot).wait_recv()
    project(0, 1)
    for slot in (1, 3, 5):
        for which in range(2):
            for s in (slot, slot + 1):
                a_copy(s, which).wait_recv()
                if s + 2 < 7:
                    a_copy(s + 2, which).start()
                elif (s, which) in ((5, 0), (6, 1)):
                    a_copy(7, which).start()
        project(slot, 2)
    a_copy(7, 0).wait_recv()
    a_copy(7, 1).wait_recv()
    project(7, 1)

    def f_copy(spot):
        row = (spot % 2) * TOK + core * HALF
        return remote(
            fb.at[spot], fin.at[pl.ds(pl.multiple_of(row, HALF), HALF)],
            f_ss.at[spot], f_rs.at[spot % 2, core], out_device(spot // 2),
        )

    for spot in range(4):
        @pl.loop(0, YL * NX)
        def _(source):
            @pl.when(source != chip)
            def _():
                remote(
                    cb.at[0, 0], rb.at[source, spot], c_ss.at[0, 0], c_rs.at[source, spot], sibling
                ).wait_recv()

        summed = rb[0, spot].astype(F32)
        for source in range(1, YL * NX):
            summed += rb[source, spot].astype(F32)
        fb[spot] = summed.astype(BF16)
        f_copy(spot).start()

    for spot in range(2):
        for from_core in range(CORES):
            row = spot * TOK + from_core * HALF
            remote(
                fb.at[0], fin.at[row : row + HALF], f_ss.at[0], f_rs.at[spot, from_core], sibling
            ).wait_recv()
    o_ref[...] = fin[...]

    for which in range(2):
        for slot in range(1, NZ):
            kv_copy(slot, which).wait_send()
            a_copy(slot, which).wait_send()
    for slot in range(1, YH):
        for half in range(2):
            q_copy(slot, half).wait_send()
            w_copy(slot, half).wait_send()
    for slot in range(YH):
        sib_copy(slot).wait_send()
        for which in range(CORES):
            if (slot, which) != (0, 0):
                for copy in o_copies(slot, which):
                    copy.wait_send()
    for slot in range(NZ):
        for w_slot in range(YH):
            to_yl, to_x, _ = c_place(slot, w_slot)

            @pl.when(to_yl * NX + to_x != chip)
            def _():
                c_copy(slot, w_slot).wait_send()
    for spot in range(4):
        f_copy(spot).wait_send()


def body(queries, suffix_kv, cache_pool, hit_count, hit_slots, out_weight):
    hits = hit_count[lax.axis_index("ctx")]
    slots = hit_slots[0]
    kept = jnp.arange(HCAP, dtype=jnp.int32) < hits
    key_blocks = jnp.take(cache_pool[0], jnp.where(kept, slots, slots[0]), axis=0)
    value_blocks = jnp.take(cache_pool[1], slots, axis=0)
    value_blocks = jnp.where(kept[:, None, None], value_blocks, jnp.zeros((), BF16))
    keys = jnp.concatenate([key_blocks.reshape(HCAP * BLK, HD), suffix_kv[0]], axis=0)
    values = jnp.concatenate([value_blocks.reshape(HCAP * BLK, HD), suffix_kv[1]], axis=0)
    vmem = pl.BlockSpec(memory_space=pltpu.VMEM)
    dma = pltpu.SemaphoreType.DMA
    return pl.pallas_call(
        kernel,
        out_shape=jax.ShapeDtypeStruct((2 * TOK, COLS), BF16),
        in_specs=[vmem] * 4 + [pl.BlockSpec(memory_space=pltpu.SMEM)],
        out_specs=vmem,
        scratch_shapes=[
            pltpu.VMEM((NZ, KEYS, HD), BF16),
            pltpu.VMEM((NZ, KEYS, HD), BF16),
            pltpu.VMEM((YH, WIDTH, HD), BF16),
            pltpu.VMEM((CORES, YH, WIDTH, COLS), BF16),
            pltpu.VMEM((YH, WIDTH, 2 * HD), F32),
            pltpu.VMEM((YH, WIDTH, HD), F32),
            pltpu.VMEM((YH, CORES, HALF, WIDTH), BF16),
            pltpu.VMEM((YH, 16, TOK), F32),
            pltpu.VMEM((CORES, YH, HALF, WIDTH), BF16),
            pltpu.VMEM((CORES, YH, 16, TOK), F32),
            pltpu.VMEM((TOK, HD), F32),
            pltpu.VMEM((NZ, CORES, HALF, WIDTH), BF16),
            pltpu.VMEM((NZ, YH, HALF, COLS), BF16),
            pltpu.VMEM((YL * NX, 4, HALF, COLS), BF16),
            pltpu.VMEM((4, HALF, COLS), BF16),
            pltpu.VMEM((2 * TOK, COLS), BF16),
            dma((NZ, 2)), dma((NZ, 2)),
            dma((YH, 2)), dma((YH, 2)),
            dma((YH, 2)), dma((YH, 2)),
            dma((YH,)), dma((YH,)),
            dma((YH, 2)), dma((YH, 2)),
            dma((YH, 2)), dma((YH, 2)),
            dma((NZ, 2)), dma((NZ, 2)),
            dma((NZ, YH)), dma((YL * NX, 4)),
            dma((4,)), dma((2, CORES)),
        ],
        compiler_params=pltpu.CompilerParams(
            collective_id=0, has_side_effects=True, vmem_limit_bytes=48 << 20
        ),
        cost_estimate=pl.CostEstimate(
            flops=6_000_000_000, bytes_accessed=1_000_000, transcendentals=8_400_000
        ),
        name="attention_and_projection",
    )(queries, keys, values, out_weight, hit_count)


def solution(mesh):
    placed = (
        P("ctx", "tp"),
        P(None, "ctx", "tp"),
        P(None, "ctx", None, "tp"),
        P(),
        P("ctx", None),
        P("tp", "ctx"),
    )
    return jax.shard_map(
        body, mesh=mesh, in_specs=placed, out_specs=P("tp", "ctx"), check_vma=False
    )
```

time: 421 us -> 113 us (0.27)
  the two profiles are of different devices: /device:TPU:16 before, /device:TPU:2 now
where the time goes in v1:
time: 113 us; the launch traced here: 112 us
  Pallas kernels  104 us (92%)
  local copies, waits for them, and re-layouts  6.65 us (6%)
  other arithmetic  1.54 us (1%)
    pallas_call x1, Pallas kernels, body(): pl.pallas_call(kernel, out_shape=jax.ShapeDtypeStruct((2 * TOK, COLS), BF...  104 us
    unnamed x11, local copies, waits for them, and re-layouts  3.66 us

profile of v1, /device:TPU:2, one launch (start us, length us, event | category | flops | bytes accessed | tf_op | source)
XLA Modules:
  0.0 112.2 jit_solution(11431903415431018963)
XLA Ops:
  0.0 0.0 copy-start.2
  0.0 0.7 copy-done.2
  0.7 0.6 dynamic_slice.3
  1.2 0.0 copy-start.4
  1.2 0.7 copy-done.4
  1.9 0.7 compare_and_fusion.1
  2.6 1.3 %slice_bitcast_fusion = (bf16[16,128,128]{2,1,0:T(8,128)(2,1)S(1)}, bf16[16,128,128]{2,1,0:T(8,128)(2,1)S(1)}) fusion(bf16[2,16,128,128]{3,2,1,0:T(8,128)(2,1)} %param.10), kind=kLoop, calls=%fused_computation.2 | loop fusion | bytes 2097152 | tf_op jit(solution)/shard_map/squeeze | solution.py:414
  3.9 0.6 gather_fusion
  4.5 0.1 broadcast_select_fusion
  4.5 0.6 iota_compare_fusion
  5.2 0.6 gather_fusion.1
  5.8 0.0 copy-start.3
  5.8 0.1 select_select_fusion
  5.9 0.7 copy-done.3
  6.6 0.0 copy-start
  6.6 0.0 copy-start.1
  6.7 0.9 copy-done
  7.6 0.0 copy-done.1
  7.6 103.9 %attention_and_projection.1 = bf16[256,256]{1,0:T(8,128)(2,1)S(1)} custom-call(bf16[128,512]{1,0:T(8,128)(2,1)S(1)} %copy-done.1, bf16[512,128]{1,0:T(8,128)(2,1)S(1)} %get-tuple-element.13.k_ref, bf16[512,128]{1,0:T(8,128)(2,1)S(1)} %get-tuple-element.14.v_ref, bf16[512,256]{1,0:T(8,128)(2,1)S(1)} %copy-done, s32[32]{0:T(128)S(1)} %copy-done.2), custom_call_target="tpu_custom_call" | custom-call | flops 6000000000 | bytes 1000000 | tf_op jit(solution)/shard_map/attention_and_projection/pallas_call | solution.py:420
  111.6 0.7 copy.8
  (5 shorter events, 0.0 us)
Async XLA Ops:
  0.0 0.7 copy-start.2
  1.2 0.7 copy-start.4
  5.8 0.8 copy-start.3
  6.6 0.9 copy-start
  6.6 1.0 copy-start.1

commit v2 on v1

--- a/solution.py
+++ b/solution.py
@@ -31,9 +31,9 @@
 
 
 def kernel(
-    q_ref, k_ref, v_ref, w_ref, count_ref, o_ref,
-    kb, vb, qb, wb, acc, mx, ob, st, rob, rst, wt, ab, cb, rb, fb, fin,
-    k_ss, k_rs, q_ss, q_rs, w_ss, w_rs, s_ss, s_rs, o_ss, o_rs, t_ss, t_rs, a_ss, a_rs,
+    q_hbm, suffix_hbm, pool_hbm, w_hbm, count_ref, slots_ref, o_ref,
+    q_ref, suffix_ref, pool_ref, kb, vb, qb, wb, acc, mx, ob, st, rob, rst, wt, ab, cb, rb, fb, fin,
+    in_s, k_ss, k_rs, q_ss, q_rs, w_ss, w_rs, s_ss, s_rs, o_ss, o_rs, t_ss, t_rs, a_ss, a_rs,
     c_ss, c_rs, f_ss, f_rs,
 ):
     c_index = lax.axis_index("ctx")
@@ -65,6 +65,14 @@
     def out_device(to_core):
         return at(out_y, z, yh // 2, (yh % 2) * 2 + x % 2, to_core)
 
+    loads = [
+        pltpu.make_async_copy(pool_hbm, pool_ref, in_s.at[0]),
+        pltpu.make_async_copy(suffix_hbm, suffix_ref, in_s.at[1]),
+        pltpu.make_async_copy(q_hbm, q_ref, in_s.at[2]),
+        pltpu.make_async_copy(w_hbm, wb.at[0, 0], in_s.at[3]),
+    ]
+    for load in loads:
+        load.start()
     barrier = pltpu.get_barrier_semaphore()
     greeted = [z_right, z_left, sibling]
     for step in range(1, YH):
@@ -123,31 +131,41 @@
         lax.broadcasted_iota(jnp.int32, (2 * TOK, TOK), 1)
     )
 
-    def absorb(q_slot, step_y, slot, count, step_z):
+    def y_step(slot):
+        if isinstance(slot, int):
+            return Y_STEP[slot]
+        return (slot * 3 + (slot // 2) * 3 + (slot // 3) * 2) % YH
+
+    def absorb(q_slots, slot, count):
         ones = []
-        gaps = []
+        z_keys = []
         for i in range(count):
-            z_key = (z + step_z[i]) % NZ
+            z_key = (z + Z_STEP[slot + i]) % NZ
+            z_keys.append(z_key)
             hits = count_ref[yh * NZ + z_key]
             for b in range(HCAP):
                 ones.append(jnp.full((BLK, HD), jnp.where(b < hits, 1.0, 0.0), F32).astype(BF16))
             ones.append(jnp.ones((TOK, HD), BF16))
-            gaps.append(((yh + step_y) % YH * NZ + z - yh * NZ - z_key) * TOK)
         ones = jnp.concatenate(ones, axis=0)
         keys = kb[slot : slot + count].reshape(count * KEYS, HD)
         values = jnp.concatenate([vb[slot : slot + count].reshape(count * KEYS, HD), ones], axis=1)
-
-        @pl.loop(0, HEADS // 2)
-        def _(pair):
-            rows = pl.ds(pl.multiple_of(pair * 2 * TOK, 2 * TOK), 2 * TOK)
-            scores = lax.dot_general(
-                qb[q_slot, rows, :], keys, (((1,), (1,)), ((), ())), preferred_element_type=F32
+        blocks = [(q_slot, pair) for q_slot in q_slots for pair in range(HEADS // 2)]
+        all_scores = [
+            lax.dot_general(
+                qb[q_slot, pair * 2 * TOK : (pair + 1) * 2 * TOK, :], keys,
+                (((1,), (1,)), ((), ())), preferred_element_type=F32,
             )
+            for q_slot, pair in blocks
+        ]
+        for (q_slot, pair), scores in zip(blocks, all_scores):
+            rows = slice(pair * 2 * TOK, (pair + 1) * 2 * TOK)
+            y_query = (yh + y_step(q_slot)) % YH
             parts = []
             for i in range(count):
+                gap = ((y_query - yh) * NZ + z - z_keys[i]) * TOK
                 parts.append(scores[:, i * KEYS : i * KEYS + HCAP * BLK])
                 own = scores[:, i * KEYS + HCAP * BLK : (i + 1) * KEYS]
-                parts.append(jnp.where(row_minus_col + gaps[i] >= 0, own, NEG))
+                parts.append(jnp.where(row_minus_col + gap >= 0, own, NEG))
             scores = jnp.concatenate(parts, axis=1)
             before = mx[q_slot, rows, :]
             now = jnp.maximum(before, jnp.max(scores, axis=1, keepdims=True))
@@ -159,16 +177,26 @@
                 acc[q_slot, rows, :] * jnp.concatenate([fade, fade], axis=1) + mixed
             )
 
-    kb[0] = k_ref[...]
-    vb[0] = v_ref[...]
+    loads[0].wait()
+    loads[1].wait()
+    hits = count_ref[c_index]
+    for b in range(HCAP):
+        rows = slice(b * BLK, (b + 1) * BLK)
+        kept = b < hits
+        kb[0, rows, :] = pool_ref[0, jnp.where(kept, slots_ref[0, b], slots_ref[0, 0])]
+        keep = jnp.full((BLK, HD), jnp.where(kept, 1.0, 0.0), F32).astype(BF16)
+        vb[0, rows, :] = pool_ref[1, slots_ref[0, b]] * keep
+    kb[0, HCAP * BLK :, :] = suffix_ref[0]
+    vb[0, HCAP * BLK :, :] = suffix_ref[1]
     for which in range(2):
         for slot in (1, 2):
             kv_copy(slot, which).start()
+    loads[2].wait()
     for head in range(HEADS):
         qb[0, head * TOK : (head + 1) * TOK, :] = q_ref[:, head * HD : (head + 1) * HD]
     for slot, half in ((1, 0), (2, 1), (1, 1), (2, 0)):
         q_copy(slot, half).start()
-    wb[0, 0] = w_ref[...]
+    loads[3].wait()
     sib_copy(0).start()
 
     @pl.loop(0, YH)
@@ -185,12 +213,9 @@
                 elif (s, which) in ((5, 0), (6, 1)):
                     kv_copy(7, which).start()
 
-    def y_step(slot):
-        return (slot * 5 - slot * slot * 2) % YH if not isinstance(slot, int) else Y_STEP[slot]
-
-    absorb(0, 0, 0, 1, Z_STEP[0:1])
+    absorb([0], 0, 1)
     pass_on(1)
-    absorb(0, 0, 1, 2, Z_STEP[1:3])
+    absorb([0], 1, 2)
     q_copy(1, 0).wait_recv()
     q_copy(3, 0).start()
     q_copy(2, 1).wait_recv()
@@ -201,26 +226,20 @@
         w_copy(slot, half).start()
     pass_on(3)
 
-    @pl.loop(1, 3)
-    def _(slot):
-        step = 3 - 2 * (slot - 1)
-        absorb(slot, step, 0, 1, Z_STEP[0:1])
-        absorb(slot, step, 1, 2, Z_STEP[1:3])
+    absorb([1, 2], 0, 3)
 
     @pl.loop(0, 3)
     def _(slot):
-        absorb(slot, (slot * 3 + (slot // 2) * 3) % YH, 3, 2, Z_STEP[3:5])
+        absorb([slot], 3, 2)
 
     pass_on(5)
     q_copy(3, 0).wait_recv()
     q_copy(3, 1).wait_recv()
-    absorb(3, 2, 0, 1, Z_STEP[0:1])
-    absorb(3, 2, 1, 2, Z_STEP[1:3])
-    absorb(3, 2, 3, 2, Z_STEP[3:5])
-
-    @pl.loop(0, YH)
-    def _(slot):
-        absorb(slot, (slot * 3 + (slot // 2) * 3 + (slot // 3) * 2) % YH, 5, 2, Z_STEP[5:7])
+    absorb([3], 0, 5)
+
+    @pl.loop(0, 2)
+    def _(pair):
+        absorb([2 * pair, 2 * pair + 1], 5, 2)
 
     w_copy(1, 0).wait_recv()
     w_copy(3, 0).start()
@@ -262,13 +281,14 @@
             ),
         )
 
-    for slot in (3, 1, 2, 0):
-        absorb(slot, Y_STEP[slot], 7, 1, Z_STEP[7:8])
-        finish(slot)
-        for which in range(CORES):
-            if (slot, which) != (0, 0):
-                for copy in o_copies(slot, which):
-                    copy.start()
+    for pair in ((3, 1), (2, 0)):
+        absorb(pair, 7, 1)
+        for slot in pair:
+            finish(slot)
+            for which in range(CORES):
+                if (slot, which) != (0, 0):
+                    for copy in o_copies(slot, which):
+                        copy.start()
     rst[0, 0] = st[0]
     rob[0, 0] = ob[0, core]
     w_copy(3, 0).wait_recv()
@@ -407,22 +427,19 @@
 
 
 def body(queries, suffix_kv, cache_pool, hit_count, hit_slots, out_weight):
-    hits = hit_count[lax.axis_index("ctx")]
-    slots = hit_slots[0]
-    kept = jnp.arange(HCAP, dtype=jnp.int32) < hits
-    key_blocks = jnp.take(cache_pool[0], jnp.where(kept, slots, slots[0]), axis=0)
-    value_blocks = jnp.take(cache_pool[1], slots, axis=0)
-    value_blocks = jnp.where(kept[:, None, None], value_blocks, jnp.zeros((), BF16))
-    keys = jnp.concatenate([key_blocks.reshape(HCAP * BLK, HD), suffix_kv[0]], axis=0)
-    values = jnp.concatenate([value_blocks.reshape(HCAP * BLK, HD), suffix_kv[1]], axis=0)
     vmem = pl.BlockSpec(memory_space=pltpu.VMEM)
+    hbm = pl.BlockSpec(memory_space=pl.ANY)
+    smem = pl.BlockSpec(memory_space=pltpu.SMEM)
     dma = pltpu.SemaphoreType.DMA
     return pl.pallas_call(
         kernel,
         out_shape=jax.ShapeDtypeStruct((2 * TOK, COLS), BF16),
-        in_specs=[vmem] * 4 + [pl.BlockSpec(memory_space=pltpu.SMEM)],
+        in_specs=[hbm] * 4 + [smem] * 2,
         out_specs=vmem,
         scratch_shapes=[
+            pltpu.VMEM(queries.shape, BF16),
+            pltpu.VMEM(suffix_kv.shape, BF16),
+            pltpu.VMEM(cache_pool.shape, BF16),
             pltpu.VMEM((NZ, KEYS, HD), BF16),
             pltpu.VMEM((NZ, KEYS, HD), BF16),
             pltpu.VMEM((YH, WIDTH, HD), BF16),
@@ -439,6 +456,7 @@
             pltpu.VMEM((YL * NX, 4, HALF, COLS), BF16),
             pltpu.VMEM((4, HALF, COLS), BF16),
             pltpu.VMEM((2 * TOK, COLS), BF16),
+            dma((4,)),
             dma((NZ, 2)), dma((NZ, 2)),
             dma((YH, 2)), dma((YH, 2)),
             dma((YH, 2)), dma((YH, 2)),
@@ -450,13 +468,13 @@
             dma((4,)), dma((2, CORES)),
         ],
         compiler_params=pltpu.CompilerParams(
-            collective_id=0, has_side_effects=True, vmem_limit_bytes=48 << 20
+            collective_id=0, has_side_effects=True, vmem_limit_bytes=62 << 20
         ),
         cost_estimate=pl.CostEstimate(
             flops=6_000_000_000, bytes_accessed=1_000_000, transcendentals=8_400_000
         ),
         name="attention_and_projection",
-    )(queries, keys, values, out_weight, hit_count)
+    )(queries, suffix_kv, cache_pool, out_weight, hit_count, hit_slots)
 
 
 def solution(mesh):

time: 113 us -> 92.3 us (0.82)
  Pallas kernels: 104 us -> 89.9 us
  local copies, waits for them, and re-layouts: 6.65 us -> 1.57 us
  other arithmetic: 1.54 us -> 0 us
    pallas_call x1, Pallas kernels: 104 us -> 89.9 us  [body(): pl.pallas_call(kernel, out_shape=jax.ShapeDtypeStruct((2 * TOK, COLS), BF...]
    unnamed x11 -> x1, local copies, waits for them, and re-layouts: 3.66 us -> 1.57 us
    squeeze x2 -> x0, local copies, waits for them, and re-layouts: 1.28 us -> none  [the longest x1 1.27 us: body(): value_blocks = jnp.take(cache_pool[1], slots, axis=0)]
    gather x2 -> x0, local copies, waits for them, and re-layouts: 1.13 us -> none  [the longest x1 0.57 us: body(): jnp.take(cache_pool[0], jnp.where(kept, slots, slots[0]), axis=0)]
where the time goes in v2:
time: 92.3 us; the launch traced here: 91.5 us
  Pallas kernels  89.9 us (97%)
  local copies, waits for them, and re-layouts  1.57 us (2%)
    pallas_call x1, Pallas kernels, body(): pl.pallas_call(kernel, out_shape=jax.ShapeDtypeStruct((2 * TOK, COLS), BF...  89.9 us

profile of v2, /device:TPU:2, one launch (start us, length us, event | category | flops | bytes accessed | tf_op | source)
XLA Modules:
  0.0 91.5 jit_solution(16023392302938945669)
XLA Ops:
  0.0 89.9 %attention_and_projection.1 = bf16[256,256]{1,0:T(8,128)(2,1)} custom-call(bf16[128,512]{1,0:T(8,128)(2,1)} %q_hbm.1, bf16[2,128,128]{2,1,0:T(8,128)(2,1)} %suffix_hbm.1, bf16[2,16,128,128]{3,2,1,0:T(8,128)(2,1)} %pool_hbm.1, bf16[512,256]{1,0:T(8,128)(2,1)} %w_hbm.1, s32[32]{0:T(128)} %count_ref.1, s32[1,3]{1,0:T(1,128)} %slots_ref.1), custom_call_target="tpu_custom_call" | custom-call | flops 6000000000 | bytes 1000000 | tf_op jit(solution)/shard_map/attention_and_projection/pallas_call | solution.py:434
  89.9 1.6 %copy.8 = bf16[256,256]{1,0:T(8,128)(2,1)} copy(bf16[256,256]{1,0:T(8,128)(2,1)} %attention_and_projection.1) | data formatting | bytes 262144

commit v3 on v2

--- a/solution.py
+++ b/solution.py
@@ -15,6 +15,8 @@
 TOK = 128
 KEYS = HCAP * BLK + TOK
 HALF = TOK // CORES
+GROUPS = 4
+PART = HALF // GROUPS
 WIDTH = HEADS * HD
 COLS = 256
 NEG = -1e30
@@ -65,14 +67,6 @@
     def out_device(to_core):
         return at(out_y, z, yh // 2, (yh % 2) * 2 + x % 2, to_core)
 
-    loads = [
-        pltpu.make_async_copy(pool_hbm, pool_ref, in_s.at[0]),
-        pltpu.make_async_copy(suffix_hbm, suffix_ref, in_s.at[1]),
-        pltpu.make_async_copy(q_hbm, q_ref, in_s.at[2]),
-        pltpu.make_async_copy(w_hbm, wb.at[0, 0], in_s.at[3]),
-    ]
-    for load in loads:
-        load.start()
     barrier = pltpu.get_barrier_semaphore()
     greeted = [z_right, z_left, sibling]
     for step in range(1, YH):
@@ -86,26 +80,36 @@
         greeted.append(at(y_tok, z, in_yl, in_x, from_core))
     for device in greeted:
         pl.semaphore_signal(barrier, inc=1, device_id=device, device_id_type=MESH)
-    pl.semaphore_wait(barrier, len(greeted))
-
-    def kv_copy(slot, which):
+    loads = [
+        pltpu.make_async_copy(pool_hbm, pool_ref, in_s.at[0]),
+        pltpu.make_async_copy(suffix_hbm, suffix_ref, in_s.at[1]),
+        pltpu.make_async_copy(q_hbm, q_ref, in_s.at[2]),
+        pltpu.make_async_copy(w_hbm, wb.at[0, 0], in_s.at[3]),
+    ]
+    for load in loads:
+        load.start()
+
+    def kv_copy(slot, which, part):
         buf = (kb, vb)[which]
+        rows = pl.ds(part * (KEYS // 2), KEYS // 2)
         if slot == 7:
             source, device = (5, z_right) if which == 0 else (6, z_left)
         else:
             source, device = max(slot - 2, 0), z_right if slot % 2 else z_left
         return remote(
-            buf.at[source], buf.at[slot], k_ss.at[slot, which], k_rs.at[slot, which], device
-        )
-
-    def a_copy(slot, which):
+            buf.at[source, rows], buf.at[slot, rows],
+            k_ss.at[slot, which, part], k_rs.at[slot, which, part], device,
+        )
+
+    def a_copy(slot, group, which):
         if slot == 7:
             source, device = (5, z_right) if which == 0 else (6, z_left)
+            src, dst = ab.at[source, group, which], ab.at[slot, group, which]
         else:
             source, device = max(slot - 2, 0), z_right if slot % 2 else z_left
+            src, dst = ab.at[source, group], ab.at[slot, group]
         return remote(
-            ab.at[source, which], ab.at[slot, which],
-            a_ss.at[slot, which], a_rs.at[slot, which], device,
+            src, dst, a_ss.at[slot, group, which], a_rs.at[slot, group, which], device
         )
 
     def y_copy(buf, ss, rs, slot, half):
@@ -188,12 +192,14 @@
         vb[0, rows, :] = pool_ref[1, slots_ref[0, b]] * keep
     kb[0, HCAP * BLK :, :] = suffix_ref[0]
     vb[0, HCAP * BLK :, :] = suffix_ref[1]
-    for which in range(2):
-        for slot in (1, 2):
-            kv_copy(slot, which).start()
     loads[2].wait()
     for head in range(HEADS):
         qb[0, head * TOK : (head + 1) * TOK, :] = q_ref[:, head * HD : (head + 1) * HD]
+    pl.semaphore_wait(barrier, len(greeted))
+    for which in range(2):
+        for part in range(2):
+            for slot in (1, 2):
+                kv_copy(slot, which, part).start()
     for slot, half in ((1, 0), (2, 1), (1, 1), (2, 0)):
         q_copy(slot, half).start()
     loads[3].wait()
@@ -206,12 +212,13 @@
 
     def pass_on(slot):
         for which in range(2):
-            for s in (slot, slot + 1):
-                kv_copy(s, which).wait_recv()
-                if s + 2 < 7:
-                    kv_copy(s + 2, which).start()
-                elif (s, which) in ((5, 0), (6, 1)):
-                    kv_copy(7, which).start()
+            for part in range(2):
+                for s in (slot, slot + 1):
+                    kv_copy(s, which, part).wait_recv()
+                    if s + 2 < 7:
+                        kv_copy(s + 2, which, part).start()
+                    elif (s, which) in ((5, 0), (6, 1)):
+                        kv_copy(7, which, part).start()
 
     absorb([0], 0, 1)
     pass_on(1)
@@ -249,8 +256,9 @@
     sib_copy(1).start()
     w_copy(2, 0).wait_recv()
     sib_copy(2).start()
-    kv_copy(7, 0).wait_recv()
-    kv_copy(7, 1).wait_recv()
+    for which in range(2):
+        for part in range(2):
+            kv_copy(7, which, part).wait_recv()
 
     lane = lax.broadcasted_iota(jnp.int32, (TOK, HD), 1)
 
@@ -260,66 +268,88 @@
             rows = slice(head * TOK, (head + 1) * TOK)
             total = acc[slot, rows, HD:]
             result = (acc[slot, rows, :HD] / total).astype(BF16)
-            for half in range(CORES):
-                ob[slot, half, :, head * HD : (head + 1) * HD] = (
-                    result[half * HALF : (half + 1) * HALF]
-                )
+            for to_core in range(CORES):
+                for group in range(GROUPS):
+                    row = to_core * HALF + group * PART
+                    ob[slot, to_core, group, :, head * HD : (head + 1) * HD] = (
+                        result[row : row + PART]
+                    )
             stats = jnp.where(lane == head, mx[slot, rows, :] * SCALE, stats)
             stats = jnp.where(lane == 8 + head, total, stats)
         st[slot] = stats.T[:16, :]
 
-    def o_copies(slot, which):
+    def o_copies(slot, which, group):
         to_core = (core, other)[which]
         device = at((yh + Y_STEP[slot]) % YH, z, yl, x, to_core)
-        return (
+        copies = []
+        if group == 0:
+            copies.append(
+                remote(
+                    st.at[slot], rst.at[which, slot],
+                    t_ss.at[slot, which], t_rs.at[slot, which], device,
+                )
+            )
+        copies.append(
             remote(
-                st.at[slot], rst.at[which, slot], t_ss.at[slot, which], t_rs.at[slot, which], device
-            ),
-            remote(
-                ob.at[slot, to_core], rob.at[which, slot],
-                o_ss.at[slot, which], o_rs.at[slot, which], device,
-            ),
-        )
+                ob.at[slot, to_core, group], rob.at[which, slot, group],
+                o_ss.at[slot, which, group], o_rs.at[slot, which, group], device,
+            )
+        )
+        return copies
+
+    def all_o_copies(slots, group):
+        return [
+            copy
+            for slot in slots
+            for which in range(CORES)
+            if (slot, which) != (0, 0)
+            for copy in o_copies(slot, which, group)
+        ]
 
     for pair in ((3, 1), (2, 0)):
         absorb(pair, 7, 1)
         for slot in pair:
             finish(slot)
-            for which in range(CORES):
-                if (slot, which) != (0, 0):
-                    for copy in o_copies(slot, which):
-                        copy.start()
+            for copy in all_o_copies([slot], 0):
+                copy.start()
+    for group in range(1, GROUPS):
+        for copy in all_o_copies((3, 1, 2, 0), group):
+            copy.start()
     rst[0, 0] = st[0]
     rob[0, 0] = ob[0, core]
     w_copy(3, 0).wait_recv()
     w_copy(3, 1).wait_recv()
     sib_copy(3).start()
-    for slot in (3, 1, 2, 0):
+
+    for group in range(GROUPS):
+        for copy in all_o_copies((3, 1, 2, 0), group):
+            copy.wait_recv()
+        if group == 0:
+            shares = []
+            for which in range(CORES):
+                top = rst[which, 0, :8]
+                for slot in range(1, YH):
+                    top = jnp.maximum(top, rst[which, slot, :8])
+                raw = [
+                    rst[which, slot, 8:] * jnp.exp2(rst[which, slot, :8] - top)
+                    for slot in range(YH)
+                ]
+                whole = raw[0] + raw[1] + raw[2] + raw[3]
+                shares += [share / whole for share in raw]
+            wt[...] = jnp.concatenate(shares + shares, axis=0).T
+        share = wt[pl.ds(pl.multiple_of(core * HALF + group * PART, PART), PART), :]
         for which in range(CORES):
-            if (slot, which) != (0, 0):
-                for copy in o_copies(slot, which):
-                    copy.wait_recv()
-
-    shares = []
-    for which in range(CORES):
-        top = rst[which, 0, :8]
-        for slot in range(1, YH):
-            top = jnp.maximum(top, rst[which, slot, :8])
-        raw = [rst[which, slot, 8:] * jnp.exp2(rst[which, slot, :8] - top) for slot in range(YH)]
-        whole = raw[0] + raw[1] + raw[2] + raw[3]
-        shares += [share / whole for share in raw]
-    wt[...] = jnp.concatenate(shares + shares, axis=0).T
-    share = wt[pl.ds(pl.multiple_of(core * HALF, HALF), HALF), :]
-    for which in range(CORES):
-        for head in range(HEADS):
-            columns = slice(head * HD, (head + 1) * HD)
-            summed = jnp.zeros((HALF, HD), F32)
-            for slot in range(YH):
-                spot = (which * YH + slot) * 8 + head
-                summed += share[:, spot : spot + 1] * rob[which, slot, :, columns].astype(F32)
-            ab[0, which, :, columns] = summed.astype(BF16)
+            for head in range(HEADS):
+                columns = slice(head * HD, (head + 1) * HD)
+                summed = jnp.zeros((PART, HD), F32)
+                for slot in range(YH):
+                    spot = (which * YH + slot) * 8 + head
+                    summed += (
+                        share[:, spot : spot + 1] * rob[which, slot, group, :, columns].astype(F32)
+                    )
+                ab[0, group, which, :, columns] = summed.astype(BF16)
         for slot in (1, 2):
-            a_copy(slot, which).start()
+            a_copy(slot, group, 0).start()
 
     def c_place(slot, w_slot):
         step = Y_STEP[w_slot]
@@ -337,7 +367,10 @@
         )
 
     def project(slot, count):
-        left = [ab[slot : slot + count, which].reshape(count * HALF, WIDTH) for which in range(CORES)]
+        left = [
+            ab[slot : slot + count, :, which].reshape(count * HALF, WIDTH)
+            for which in range(CORES)
+        ]
         for w_slot in (3, 1, 2, 0):
             part = jnp.dot(left[0], wb[0, w_slot], preferred_element_type=F32)
             part += jnp.dot(left[1], wb[1, w_slot], preferred_element_type=F32)
@@ -355,21 +388,13 @@
                 def _():
                     c_copy(slot + i, w_slot).start()
 
-    for slot in range(YH):
-        sib_copy(slot).wait_recv()
-    project(0, 1)
-    for slot in (1, 3, 5):
-        for which in range(2):
-            for s in (slot, slot + 1):
-                a_copy(s, which).wait_recv()
-                if s + 2 < 7:
-                    a_copy(s + 2, which).start()
-                elif (s, which) in ((5, 0), (6, 1)):
-                    a_copy(7, which).start()
-        project(slot, 2)
-    a_copy(7, 0).wait_recv()
-    a_copy(7, 1).wait_recv()
-    project(7, 1)
+    def pass_a(slot, group):
+        for s in (slot, slot + 1):
+            a_copy(s, group, 0).wait_recv()
+            if s + 2 < 7:
+                a_copy(s + 2, group, 0).start()
+            else:
+                a_copy(7, group, s - 5).start()
 
     def f_copy(spot):
         row = (spot % 2) * TOK + core * HALF
@@ -378,20 +403,51 @@
             f_ss.at[spot], f_rs.at[spot % 2, core], out_device(spot // 2),
         )
 
-    for spot in range(4):
-        @pl.loop(0, YL * NX)
-        def _(source):
-            @pl.when(source != chip)
-            def _():
-                remote(
-                    cb.at[0, 0], rb.at[source, spot], c_ss.at[0, 0], c_rs.at[source, spot], sibling
-                ).wait_recv()
-
-        summed = rb[0, spot].astype(F32)
-        for source in range(1, YL * NX):
-            summed += rb[source, spot].astype(F32)
-        fb[spot] = summed.astype(BF16)
-        f_copy(spot).start()
+    def reduce(slot):
+        z_tok = (z + Z_STEP[slot]) % NZ
+        spot = z_tok % 4
+
+        @pl.when(z_tok // 4 == x % 2)
+        def _():
+            @pl.loop(0, YL * NX)
+            def _(source):
+                @pl.when(source != chip)
+                def _():
+                    remote(
+                        cb.at[0, 0], rb.at[source, spot],
+                        c_ss.at[0, 0], c_rs.at[source, spot], sibling,
+                    ).wait_recv()
+
+            summed = rb[0, spot].astype(F32)
+            for source in range(1, YL * NX):
+                summed += rb[source, spot].astype(F32)
+            fb[spot] = summed.astype(BF16)
+            f_copy(spot).start()
+
+    for slot in range(YH):
+        sib_copy(slot).wait_recv()
+    pass_a(1, 0)
+    project(0, 1)
+    for group in range(1, GROUPS):
+        pass_a(1, group)
+    pass_a(3, 0)
+    project(1, 2)
+    for group in range(1, GROUPS):
+        pass_a(3, group)
+    pass_a(5, 0)
+    project(3, 2)
+    for group in range(1, GROUPS):
+        pass_a(5, group)
+    reduce(0)
+    project(5, 2)
+    reduce(1)
+    reduce(2)
+    for group in range(GROUPS):
+        for which in range(2):
+            a_copy(7, group, which).wait_recv()
+    project(7, 1)
+    for slot in range(3, NZ):
+        reduce(slot)
 
     for spot in range(2):
         for from_core in range(CORES):
@@ -403,18 +459,21 @@
 
     for which in range(2):
         for slot in range(1, NZ):
-            kv_copy(slot, which).wait_send()
-            a_copy(slot, which).wait_send()
+            for part in range(2):
+                kv_copy(slot, which, part).wait_send()
+    for group in range(GROUPS):
+        for slot in range(1, NZ - 1):
+            a_copy(slot, group, 0).wait_send()
+        for which in range(2):
+            a_copy(NZ - 1, group, which).wait_send()
+        for copy in all_o_copies(range(YH), group):
+            copy.wait_send()
     for slot in range(1, YH):
         for half in range(2):
             q_copy(slot, half).wait_send()
             w_copy(slot, half).wait_send()
     for slot in range(YH):
         sib_copy(slot).wait_send()
-        for which in range(CORES):
-            if (slot, which) != (0, 0):
-                for copy in o_copies(slot, which):
-                    copy.wait_send()
     for slot in range(NZ):
         for w_slot in range(YH):
             to_yl, to_x, _ = c_place(slot, w_slot)
@@ -446,24 +505,24 @@
             pltpu.VMEM((CORES, YH, WIDTH, COLS), BF16),
             pltpu.VMEM((YH, WIDTH, 2 * HD), F32),
             pltpu.VMEM((YH, WIDTH, HD), F32),
-            pltpu.VMEM((YH, CORES, HALF, WIDTH), BF16),
+            pltpu.VMEM((YH, CORES, GROUPS, PART, WIDTH), BF16),
             pltpu.VMEM((YH, 16, TOK), F32),
-            pltpu.VMEM((CORES, YH, HALF, WIDTH), BF16),
+            pltpu.VMEM((CORES, YH, GROUPS, PART, WIDTH), BF16),
             pltpu.VMEM((CORES, YH, 16, TOK), F32),
             pltpu.VMEM((TOK, HD), F32),
-            pltpu.VMEM((NZ, CORES, HALF, WIDTH), BF16),
+            pltpu.VMEM((NZ, GROUPS, CORES, PART, WIDTH), BF16),
             pltpu.VMEM((NZ, YH, HALF, COLS), BF16),
             pltpu.VMEM((YL * NX, 4, HALF, COLS), BF16),
             pltpu.VMEM((4, HALF, COLS), BF16),
             pltpu.VMEM((2 * TOK, COLS), BF16),
             dma((4,)),
-            dma((NZ, 2)), dma((NZ, 2)),
+            dma((NZ, 2, 2)), dma((NZ, 2, 2)),
             dma((YH, 2)), dma((YH, 2)),
             dma((YH, 2)), dma((YH, 2)),
             dma((YH,)), dma((YH,)),
+            dma((YH, 2, GROUPS)), dma((YH, 2, GROUPS)),
             dma((YH, 2)), dma((YH, 2)),
-            dma((YH, 2)), dma((YH, 2)),
-            dma((NZ, 2)), dma((NZ, 2)),
+            dma((NZ, GROUPS, 2)), dma((NZ, GROUPS, 2)),
             dma((NZ, YH)), dma((YL * NX, 4)),
             dma((4,)), dma((2, CORES)),
         ],

time: 92.3 us -> 91.3 us (0.989)
  no operation moved by 1% of the time
where the time goes in v3:
time: 91.3 us; the launch traced here: 91.2 us
  Pallas kernels  89.6 us (98%)
  local copies, waits for them, and re-layouts  1.57 us (2%)
    pallas_call x1, Pallas kernels, body(): pl.pallas_call(kernel, out_shape=jax.ShapeDtypeStruct((2 * TOK, COLS), BF...  89.6 us

profile of v3, /device:TPU:2, one launch (start us, length us, event | category | flops | bytes accessed | tf_op | source)
XLA Modules:
  0.0 91.2 jit_solution(1287735679248966384)
XLA Ops:
  0.0 89.6 %attention_and_projection.1 = bf16[256,256]{1,0:T(8,128)(2,1)} custom-call(bf16[128,512]{1,0:T(8,128)(2,1)} %q_hbm.1, bf16[2,128,128]{2,1,0:T(8,128)(2,1)} %suffix_hbm.1, bf16[2,16,128,128]{3,2,1,0:T(8,128)(2,1)} %pool_hbm.1, bf16[512,256]{1,0:T(8,128)(2,1)} %w_hbm.1, s32[32]{0:T(128)} %count_ref.1, s32[1,3]{1,0:T(1,128)} %slots_ref.1), custom_call_target="tpu_custom_call" | custom-call | flops 6000000000 | bytes 1000000 | tf_op jit(solution)/shard_map/attention_and_projection/pallas_call | solution.py:493
  89.6 1.6 %copy.8 = bf16[256,256]{1,0:T(8,128)(2,1)} copy(bf16[256,256]{1,0:T(8,128)(2,1)} %attention_and_projection.1) | data formatting | bytes 262144

commit v4 on v3

--- a/solution.py
+++ b/solution.py
@@ -440,13 +440,13 @@
         pass_a(5, group)
     reduce(0)
     project(5, 2)
-    reduce(1)
-    reduce(2)
+    for slot in range(1, 5):
+        reduce(slot)
     for group in range(GROUPS):
         for which in range(2):
             a_copy(7, group, which).wait_recv()
     project(7, 1)
-    for slot in range(3, NZ):
+    for slot in range(5, NZ):
         reduce(slot)
 
     for spot in range(2):

time: 91.3 us -> 93.8 us (1.027)
  the two profiles are of different devices: /device:TPU:2 before, /device:TPU:70 now
where the time goes in v4:
time: 93.8 us; the launch traced here: 93.7 us
  Pallas kernels  92.1 us (98%)
  local copies, waits for them, and re-layouts  1.57 us (2%)
    pallas_call x1, Pallas kernels, body(): pl.pallas_call(kernel, out_shape=jax.ShapeDtypeStruct((2 * TOK, COLS), BF...  92.1 us

profile of v4, /device:TPU:70, one launch (start us, length us, event | category | flops | bytes accessed | tf_op | source)
XLA Modules:
  0.0 93.7 jit_solution(12660343180243418284)
XLA Ops:
  0.0 92.1 %attention_and_projection.1 = bf16[256,256]{1,0:T(8,128)(2,1)} custom-call(bf16[128,512]{1,0:T(8,128)(2,1)} %q_hbm.1, bf16[2,128,128]{2,1,0:T(8,128)(2,1)} %suffix_hbm.1, bf16[2,16,128,128]{3,2,1,0:T(8,128)(2,1)} %pool_hbm.1, bf16[512,256]{1,0:T(8,128)(2,1)} %w_hbm.1, s32[32]{0:T(128)} %count_ref.1, s32[1,3]{1,0:T(1,128)} %slots_ref.1), custom_call_target="tpu_custom_call" | custom-call | flops 6000000000 | bytes 1000000 | tf_op jit(solution)/shard_map/attention_and_projection/pallas_call | solution.py:493
  92.1 1.6 %copy.8 = bf16[256,256]{1,0:T(8,128)(2,1)} copy(bf16[256,256]{1,0:T(8,128)(2,1)} %attention_and_projection.1) | data formatting | bytes 262144
